TPU v7x, 32 devices: a whole 2x2x4 slice. The times are simulated.
32 devices in a mesh: grp: 2 (over x), row: 16 (over z, y, core).
Axes of the slice: x: 2, y: 2, z: 4, core: 2. Of those that a mesh axis runs over, the one named last changes fastest.
Arguments:
- right_sides: float32 [32, 512, 512], P(None, ('grp', 'row')), parts along dimension 1, may hold values from -180 to 180
- kappa_sq: float32 [512, 512], P(('grp', 'row')), parts along dimension 0, may hold values from 0.02 to 1
- inv_mass: float32 [512, 512], P(('grp', 'row')), parts along dimension 0, may hold values from 0.25 to 4
- cell_mask: int32 [512, 512], P(('grp', 'row')), parts along dimension 0, may hold values 0 or 1
- weights: bfloat16 [256, 8, 128, 512], P(('grp', 'row')), parts along dimension 0, may hold values from -0.75 to 0.75
- obs_precision: float32 [256, 128], P(('grp', 'row')), parts along dimension 0, may hold values from 0.5 to 8
- footprint: int32 [256, 8], P(('grp', 'row')), parts along dimension 0, may hold values from 0 to 255, as said below
Outputs:
- solution: float32 [32, 512, 512], P(None, ('grp', 'row')), parts along dimension 1
- residual: float32 [32, 512, 512], P(None, ('grp', 'row')), parts along dimension 1
There are 2 independent parts, one for each index of `grp`. A program takes and returns all parts, laid end to end along the dimension named above; each array names one. Nothing has to cross between parts.
Inputs may be any that keep to these rules, and one draw needn't show every extreme that they name: Tile t's footprint rows lie in the rows 16 * (t // 8) - 16 to 16 * (t // 8) + 2 * 16 - 1; rows may repeat.
All inputs are finite; a program needn't handle non-finite values. No bound on the sum of `cell_mask` on one device may be relied on, other than what follows from the above.
Results may differ from a plain program's by a relative error of at most 0.0095.
Values may be sent and summed in bfloat16 or wider, within the bound.
A program may use at most 64 MiB of HBM per device.

v0:
```python
import jax
import jax.numpy as jnp
from jax import lax
from jax.sharding import PartitionSpec as P

ITERS = 2


def shortened(value):
    return jax.tree.map(lambda a: a.astype(jnp.bfloat16) if a.dtype == jnp.float32 else a, value)


def extended_2(cells, sides, width):
    for axis, dim in sides:
        count = lax.axis_size(axis)
        ends = count - 1
        head = lax.slice_in_dim(cells, 0, width, axis=dim)
        tail = lax.slice_in_dim(cells, cells.shape[dim] - width, cells.shape[dim], axis=dim)
        cells = jnp.concatenate(
            [
                lax.ppermute(tail, axis, [(i, (i + 1) % count) for i in range(ends)]),
                cells,
                lax.ppermute(head, axis, [((i + 1) % count, i) for i in range(ends)]),
            ],
            axis=dim,
        )
    return cells


def shifted(block, axis, distance):
    devices = range(lax.axis_size(axis))
    route = [(i - distance, i) for i in devices if i - distance in devices]
    return lax.ppermute(block, axis, route)


def neighbour_sum(extended):
    padded = jnp.pad(extended, ((0, 0), (0, 0), (1, 1)))
    return padded[:, 2:, 1:-1] + padded[:, :-2, 1:-1] + padded[:, 1:-1, 2:] + padded[:, 1:-1, :-2]


def gram_matrix(left, right):
    count = left.shape[0]
    return jnp.dot(
        left.reshape(count, -1), right.reshape(count, -1).T, precision=lax.Precision.HIGHEST
    )


def solve_small(matrix, target):
    factor = jnp.linalg.cholesky(0.5 * (matrix + matrix.T))
    return jax.scipy.linalg.cho_solve((factor, True), target)


def combine(coeffs, fields):
    return jnp.einsum("jk,jrc->krc", coeffs, fields, precision=lax.Precision.HIGHEST)


def body(right_sides, kappa_sq, inv_mass, cell_mask, weights, obs_precision, footprint):
    count_rhs, own_rows, columns = right_sides.shape
    tile_count, foot_rows = footprint.shape
    maskf = cell_mask.astype(jnp.float32)
    device = lax.axis_index("row")
    local_ids = (footprint - (device * own_rows - own_rows)).reshape(-1)
    selector = (local_ids[:, None] == jnp.arange(3 * own_rows, dtype=jnp.int32)[None, :]).astype(
        jnp.float32
    )
    selector_half = selector.astype(jnp.bfloat16)

    def stencil_from(field, masked_ext):
        return kappa_sq * field + maskf * (4.0 * field - neighbour_sum(masked_ext))

    def stencil(field):
        masked_ext = extended_2(shortened(maskf * field), (("row", 1),), 1)
        return stencil_from(field, masked_ext)

    solution = jnp.zeros_like(right_sides)
    residual = right_sides
    direction = right_sides
    res_gram = lax.psum(gram_matrix(residual, residual), "row")
    for step in range(ITERS):
        half_ext = extended_2(direction.astype(jnp.bfloat16), (("row", 1),), own_rows)
        inner = stencil(direction)
        prior_part = stencil(inv_mass * inner)
        picked = jnp.einsum(
            "krc,jr->kjc", half_ext, selector_half, preferred_element_type=jnp.float32
        ).astype(jnp.bfloat16)
        picked = picked.reshape(count_rhs, tile_count, foot_rows, columns)
        observed = jnp.einsum("ktfc,tfoc->kto", picked, weights, preferred_element_type=jnp.float32)
        scaled = (obs_precision[None] * observed).astype(jnp.bfloat16)
        adjoint = jnp.einsum("kto,tfoc->ktfc", scaled, weights, preferred_element_type=jnp.float32)
        adjoint = adjoint.reshape(count_rhs, tile_count * foot_rows, columns)
        spread = jnp.einsum("kjc,jr->krc", adjoint, selector, precision=lax.Precision.HIGHEST)
        from_above = shifted(spread[:, 2 * own_rows :].astype(jnp.bfloat16), "row", 1).astype(
            jnp.float32
        )
        from_below = shifted(spread[:, :own_rows].astype(jnp.bfloat16), "row", -1).astype(
            jnp.float32
        )
        image = prior_part + spread[:, own_rows : 2 * own_rows] + from_above + from_below
        dir_gram = lax.psum(gram_matrix(direction, image), "row")
        step_size = solve_small(dir_gram, res_gram)
        solution = solution + combine(step_size, direction)
        residual = residual - combine(step_size, image)
        if step + 1 < ITERS:
            new_gram = lax.psum(gram_matrix(residual, residual), "row")
            update_mix = solve_small(res_gram, new_gram)
            direction = residual + combine(update_mix, direction)
            res_gram = new_gram
    return (solution, residual)


def solution(mesh):
    placed = (
        P(None, ("grp", "row"), None),
        P(("grp", "row"), None),
        P(("grp", "row"), None),
        P(("grp", "row"), None),
        P(("grp", "row"), None, None, None),
        P(("grp", "row"), None),
        P(("grp", "row"), None),
    )
    return jax.shard_map(
        body,
        mesh=mesh,
        in_specs=placed,
        out_specs=(P(None, ("grp", "row"), None), P(None, ("grp", "row"), None)),
        check_vma=False,
    )
```

profile of v0, /device:TPU:0, one launch (start us, length us, event | category | flops | bytes accessed | tf_op | source)
XLA Modules:
  0.0 347.0 jit_solution(2127163988441870134)
XLA Ops:
  0.7 0.8 convert_element_type.84
  1.5 1.4 multiply_convert_fusion.3
  3.0 1.3 collective-permute-start
  4.3 3.0 collective-permute-start.1
  7.3 0.9 collective-permute-done.1
  8.2 1.1 select_maximum_fusion.6
  9.3 2.4 multiply_convert_fusion.2
  11.7 1.4 collective-permute-start.5
  13.2 6.7 %collective-permute-start.4 = (bf16[32,16,512]{2,1,0:T(8,128)(2,1)S(1)}, bf16[32,16,512]{2,1,0:T(8,128)(2,1)}, u32[]{:S(2)}, u32[]{:S(2)}) collective-permute-start(bf16[32,16,512]{2,1,0:T(8,128)(2,1)S(1)} %get-tuple-element.19), channel_id=1, source_target_pairs={{0,1},{1,2},{2,3},{3,4},{4,5},{5,6},{6,7},{7,8},{8,9},{9,10},{10,1... | collective-permute-start | bytes 1572872 | tf_op jit(solution)/shard_map/ppermute | solution.py:21
  20.0 0.8 copy-done.8
  20.7 2.1 convert_bitcast_fusion.1
  22.8 11.6 %fusion.50 = f32[8,32,8,512]{3,1,2,0:T(8,128)} fusion(bf16[8,8,128,512]{3,2,1,0:T(8,128)(2,1)} %param.14, bf16[32,8,8,512]{3,2,1,0:T(8,128)(2,1)S(1)} %convert_bitcast_fusion.1, f32[8,128]{1,0:T(8,128)S(1)} %copy-done.10), kind=kOutput, calls=%fused_computation.41 | convolution fusion | flops 536936448 | bytes 14684160 | tf_op jit(solution)/shard_map/kto,tfoc->ktfc/dot_general | solution.py:89
  34.5 6.6 %fusion.116 = (bf16[32,48,512]{2,1,0:T(8,128)(2,1)S(1)}, f32[32,48,512]{2,1,0:T(8,128)S(1)}) fusion(f32[32,64,512]{2,0,1:T(8,128)} %bitcast.147, s32[64]{0:T(128)S(1)} %eq.15), kind=kOutput, calls=%fused_computation.155 | convolution fusion | flops 604769280 | bytes 8913152 | tf_op jit(solution)/shard_map/kjc,jr->krc/dot_general | solution.py:91
  41.2 1.4 collective-permute-start.7
  42.6 14.5 %collective-permute-start.6 = (bf16[32,16,512]{2,1,0:T(8,128)(2,1)S(1)}, bf16[32,16,512]{2,1,0:T(8,128)(2,1)S(1)}, u32[]{:S(2)}, u32[]{:S(2)}) collective-permute-start(bf16[32,16,512]{2,1,0:T(8,128)(2,1)S(1)} %get-tuple-element.16), channel_id=1, source_target_pairs={{0,1},{1,2},{2,3},{3,4},{4,5},{5,6},{6,7},{7,8},{8,9},{9,10},{10,1... | collective-permute-start | bytes 1572872 | tf_op jit(solution)/shard_map/ppermute | solution.py:33
  57.2 1.3 collective-permute-start.2
  58.5 5.6 %collective-permute-start.3 = (bf16[32,1,512]{2,1,0:T(2,128)(2,1)S(1)}, bf16[32,1,512]{2,1,0:T(2,128)(2,1)S(1)}, u32[]{:S(2)}, u32[]{:S(2)}) collective-permute-start(bf16[32,1,512]{2,1,0:T(2,128)(2,1)S(1)} %get-tuple-element.24), channel_id=1, source_target_pairs={{0,1},{1,2},{2,3},{3,4},{4,5},{5,6},{6,7},{7,8},{8,9},{9,10},{10,1... | collective-permute-start | bytes 98312 | tf_op jit(solution)/shard_map/ppermute | solution.py:21
  64.2 1.5 convolution_bitcast_fusion.5
  65.7 1.1 select_maximum_fusion.4
  66.8 1.3 fusion.58
  68.1 2.1 convolution_bitcast_fusion.6
  70.2 62.1 %all-reduce.4 = (f32[32,32]{1,0:T(8,128)S(1)}, f32[32,32]{1,0:T(8,128)S(1)}) all-reduce(f32[32,32]{1,0:T(8,128)S(1)} %convolution_bitcast_fusion.5, f32[32,32]{1,0:T(8,128)S(1)} %convolution_bitcast_fusion.6), channel_id=1, replica_groups=mesh['grp'=2,'row'=16] {'row'}, use_global_device_ids=true, to_apply=%region_3.5 | all-reduce | flops 2048 | bytes 16384 | tf_op jit(solution)/shard_map/psum | solution.py:78
  132.5 2.9 cholesky.59
  135.5 0.6 compare_reduce_fusion.2
  136.1 0.7 fusion.83
  136.8 2.4 custom-call.9
  139.7 1.6 fusion.65
  141.3 0.7 copy_subtract_fusion.1
  141.9 1.5 convolution_bitcast_fusion.3
  143.5 57.9 %psum.30 = f32[32,32]{1,0:T(8,128)S(1)} all-reduce(f32[32,32]{1,0:T(8,128)S(1)} %convolution_bitcast_fusion.3), channel_id=1, replica_groups=mesh['grp'=2,'row'=16] {'row'}, use_global_device_ids=true, to_apply=%region_4.7 | all-reduce | flops 1024 | bytes 8192 | tf_op jit(solution)/shard_map/psum | solution.py:104
  201.4 2.9 cholesky.70
  204.4 0.6 compare_reduce_fusion.1
  205.0 0.7 fusion.84
  205.7 2.4 custom-call.10
  208.5 1.6 fusion.68
  210.1 0.7 multiply_convert_fusion.1
  210.9 1.3 collective-permute-start.8
  212.2 3.0 collective-permute-start.9
  215.3 0.9 collective-permute-done.9
  216.2 1.1 select_maximum_fusion.2
  217.2 2.4 multiply_convert_fusion
  219.7 1.3 collective-permute-start.13
  221.0 3.3 collective-permute-start.12
  224.3 1.3 collective-permute-done.12
  225.5 2.1 convert_bitcast_fusion
  227.6 12.2 %fusion.53 = f32[8,32,8,512]{3,1,2,0:T(8,128)} fusion(bf16[8,8,128,512]{3,2,1,0:T(8,128)(2,1)} %param.14, bf16[32,8,8,512]{3,2,1,0:T(8,128)(2,1)} %convert_bitcast_fusion, f32[8,128]{1,0:T(8,128)S(1)} %copy-done.10), kind=kOutput, calls=%fused_computation.42 | convolution fusion | flops 536936448 | bytes 14684160 | tf_op jit(solution)/shard_map/kto,tfoc->ktfc/dot_general | solution.py:89
  239.8 6.6 %fusion.117 = (bf16[32,48,512]{2,1,0:T(8,128)(2,1)S(1)}, f32[32,48,512]{2,1,0:T(8,128)S(1)}) fusion(f32[32,64,512]{2,0,1:T(8,128)} %bitcast.146, s32[64]{0:T(128)S(1)} %eq.15), kind=kOutput, calls=%fused_computation.156 | convolution fusion | flops 604769280 | bytes 8913152 | tf_op jit(solution)/shard_map/kjc,jr->krc/dot_general | solution.py:91
  246.5 1.4 collective-permute-start.15
  247.9 9.7 %collective-permute-start.14 = (bf16[32,16,512]{2,1,0:T(8,128)(2,1)S(1)}, bf16[32,16,512]{2,1,0:T(8,128)(2,1)S(1)}, u32[]{:S(2)}, u32[]{:S(2)}) collective-permute-start(bf16[32,16,512]{2,1,0:T(8,128)(2,1)S(1)} %get-tuple-element.14), channel_id=1, source_target_pairs={{0,1},{1,2},{2,3},{3,4},{4,5},{5,6},{6,7},{7,8},{8,9},{9,10},{10,1... | collective-permute-start | bytes 1572872 | tf_op jit(solution)/shard_map/ppermute | solution.py:33
  257.8 1.3 collective-permute-start.10
  259.1 5.2 %collective-permute-start.11 = (bf16[32,1,512]{2,1,0:T(2,128)(2,1)S(1)}, bf16[32,1,512]{2,1,0:T(2,128)(2,1)S(1)}, u32[]{:S(2)}, u32[]{:S(2)}) collective-permute-start(bf16[32,1,512]{2,1,0:T(2,128)(2,1)S(1)} %get-tuple-element.20), channel_id=1, source_target_pairs={{0,1},{1,2},{2,3},{3,4},{4,5},{5,6},{6,7},{7,8},{8,9},{9,10},{10,1... | collective-permute-start | bytes 98312 | tf_op jit(solution)/shard_map/ppermute | solution.py:21
  264.3 2.5 fusion.70
  266.8 1.1 select_maximum_fusion
  267.9 1.3 fusion.56
  269.3 2.1 convolution_bitcast_fusion.1
  271.4 61.6 %psum.31 = f32[32,32]{1,0:T(8,128)S(1)} all-reduce(f32[32,32]{1,0:T(8,128)S(1)} %convolution_bitcast_fusion.1), channel_id=1, replica_groups=mesh['grp'=2,'row'=16] {'row'}, use_global_device_ids=true, to_apply=%region_5.8 | all-reduce | flops 1024 | bytes 8192 | tf_op jit(solution)/shard_map/psum | solution.py:99
  333.2 2.9 cholesky.81
  336.1 0.6 compare_reduce_fusion
  336.8 0.7 fusion.85
  337.4 2.4 custom-call.11
  340.3 1.6 fusion.60
  341.9 1.6 convolution_add_fusion
  343.5 1.6 copy.38
  345.1 1.6 copy_subtract_fusion
  (64 shorter events, 2.6 us)
Async XLA Ops:
  0.6 8.6 %copy-start = (f32[32,16,512]{2,1,0:T(8,128)S(1)}, f32[32,16,512]{2,1,0:T(8,128)}, u32[]{:S(2)}) copy-start(f32[32,16,512]{2,1,0:T(8,128)} %param.10) | copy-start | bytes 3145732
  0.6 8.6 %copy-start.7 = (f32[16,512]{1,0:T(8,128)S(1)}, f32[16,512]{1,0:T(8,128)}, u32[]{:S(2)}) copy-start(f32[16,512]{1,0:T(8,128)} %param.11) | copy-start | bytes 98308
  0.7 8.6 %copy-start.9 = (f32[16,512]{1,0:T(8,128)S(1)}, f32[16,512]{1,0:T(8,128)}, u32[]{:S(2)}) copy-start(f32[16,512]{1,0:T(8,128)} %param.12) | copy-start | bytes 98308
  3.0 4.3 %collective-permute-start = (bf16[32,1,512]{2,1,0:T(2,128)(2,1)S(1)}, bf16[32,1,512]{2,1,0:T(2,128)(2,1)S(1)}, u32[]{:S(2)}, u32[]{:S(2)}) collective-permute-start(bf16[32,1,512]{2,1,0:T(2,128)(2,1)S(1)} %get-tuple-element.27), channel_id=1, source_target_pairs={{1,0},{2,1},{3,2},{4,3},{5,4},{6,5},{7,6},{8,7},{9,8},{10,9},{11,1... | collective-permute-start | bytes 98312 | tf_op jit(solution)/shard_map/ppermute | solution.py:23
  4.3 3.9 %collective-permute-start.1 = (bf16[32,1,512]{2,1,0:T(2,128)(2,1)S(1)}, bf16[32,1,512]{2,1,0:T(2,128)(2,1)S(1)}, u32[]{:S(2)}, u32[]{:S(2)}) collective-permute-start(bf16[32,1,512]{2,1,0:T(2,128)(2,1)S(1)} %get-tuple-element.26), channel_id=1, source_target_pairs={{0,1},{1,2},{2,3},{3,4},{4,5},{5,6},{6,7},{7,8},{8,9},{9,10},{10,1... | collective-permute-start | bytes 98312 | tf_op jit(solution)/shard_map/ppermute | solution.py:21
  9.3 10.5 %copy-start.11 = (s32[8,8]{1,0:T(8,128)S(1)}, s32[8,8]{1,0:T(8,128)}, u32[]{:S(2)}) copy-start(s32[8,8]{1,0:T(8,128)} %param.16) | copy-start | bytes 772
  11.7 8.2 %copy-start.6 = (bf16[32,16,512]{2,1,0:T(8,128)(2,1)}, bf16[32,16,512]{2,1,0:T(8,128)(2,1)S(1)}, u32[]{:S(2)}) copy-start(bf16[32,16,512]{2,1,0:T(8,128)(2,1)S(1)} %get-tuple-element.19) | copy-start | bytes 1572868
  11.7 11.1 %copy-start.10 = (f32[8,128]{1,0:T(8,128)S(1)}, f32[8,128]{1,0:T(8,128)}, u32[]{:S(2)}) copy-start(f32[8,128]{1,0:T(8,128)} %param.15) | copy-start | bytes 12292
  11.7 8.2 %collective-permute-start.5 = (bf16[32,16,512]{2,1,0:T(8,128)(2,1)S(1)}, bf16[32,16,512]{2,1,0:T(8,128)(2,1)S(1)}, u32[]{:S(2)}, u32[]{:S(2)}) collective-permute-start(bf16[32,16,512]{2,1,0:T(8,128)(2,1)S(1)} %get-tuple-element.19), channel_id=1, source_target_pairs={{1,0},{2,1},{3,2},{4,3},{5,4},{6,5},{7,6},{8,7},{9,8},{10,9},{11,1... | collective-permute-start | bytes 1572872 | tf_op jit(solution)/shard_map/ppermute | solution.py:23
  13.2 7.6 %collective-permute-start.4 = (bf16[32,16,512]{2,1,0:T(8,128)(2,1)S(1)}, bf16[32,16,512]{2,1,0:T(8,128)(2,1)}, u32[]{:S(2)}, u32[]{:S(2)}) collective-permute-start(bf16[32,16,512]{2,1,0:T(8,128)(2,1)S(1)} %get-tuple-element.19), channel_id=1, source_target_pairs={{0,1},{1,2},{2,3},{3,4},{4,5},{5,6},{6,7},{7,8},{8,9},{9,10},{10,1... | collective-permute-start | bytes 1572872 | tf_op jit(solution)/shard_map/ppermute | solution.py:21
  19.9 0.8 copy-start.8
  41.1 16.1 %copy-start.1 = (bf16[32,16,512]{2,1,0:T(8,128)(2,1)S(1)}, bf16[32,16,512]{2,1,0:T(8,128)(2,1)}, u32[]{:S(2)}) copy-start(bf16[32,16,512]{2,1,0:T(8,128)(2,1)} %get-tuple-element.12) | copy-start | bytes 1572868
  41.1 25.7 %copy-start.4 = (f32[32,16,512]{2,1,0:T(8,128)S(1)}, f32[32,16,512]{2,1,0:T(8,128)}, u32[]{:S(2)}) copy-start(f32[32,16,512]{2,1,0:T(8,128)} %get-tuple-element.13) | copy-start | bytes 3145732
  41.2 25.6 %collective-permute-start.7 = (bf16[32,16,512]{2,1,0:T(8,128)(2,1)S(1)}, bf16[32,16,512]{2,1,0:T(8,128)(2,1)S(1)}, u32[]{:S(2)}, u32[]{:S(2)}) collective-permute-start(bf16[32,16,512]{2,1,0:T(8,128)(2,1)S(1)} %get-tuple-element.17), channel_id=1, source_target_pairs={{1,0},{2,1},{3,2},{4,3},{5,4},{6,5},{7,6},{8,7},{9,8},{10,9},{11,1... | collective-permute-start | bytes 1572872 | tf_op jit(solution)/shard_map/ppermute | solution.py:33
  42.6 24.2 %collective-permute-start.6 = (bf16[32,16,512]{2,1,0:T(8,128)(2,1)S(1)}, bf16[32,16,512]{2,1,0:T(8,128)(2,1)S(1)}, u32[]{:S(2)}, u32[]{:S(2)}) collective-permute-start(bf16[32,16,512]{2,1,0:T(8,128)(2,1)S(1)} %get-tuple-element.16), channel_id=1, source_target_pairs={{0,1},{1,2},{2,3},{3,4},{4,5},{5,6},{6,7},{7,8},{8,9},{9,10},{10,1... | collective-permute-start | bytes 1572872 | tf_op jit(solution)/shard_map/ppermute | solution.py:33
  57.2 8.4 %collective-permute-start.2 = (bf16[32,1,512]{2,1,0:T(2,128)(2,1)S(1)}, bf16[32,1,512]{2,1,0:T(2,128)(2,1)S(1)}, u32[]{:S(2)}, u32[]{:S(2)}) collective-permute-start(bf16[32,1,512]{2,1,0:T(2,128)(2,1)S(1)} %get-tuple-element.25), channel_id=1, source_target_pairs={{1,0},{2,1},{3,2},{4,3},{5,4},{6,5},{7,6},{8,7},{9,8},{10,9},{11,1... | collective-permute-start | bytes 98312 | tf_op jit(solution)/shard_map/ppermute | solution.py:23
  58.5 7.2 %collective-permute-start.3 = (bf16[32,1,512]{2,1,0:T(2,128)(2,1)S(1)}, bf16[32,1,512]{2,1,0:T(2,128)(2,1)S(1)}, u32[]{:S(2)}, u32[]{:S(2)}) collective-permute-start(bf16[32,1,512]{2,1,0:T(2,128)(2,1)S(1)} %get-tuple-element.24), channel_id=1, source_target_pairs={{0,1},{1,2},{2,3},{3,4},{4,5},{5,6},{6,7},{7,8},{8,9},{9,10},{10,1... | collective-permute-start | bytes 98312 | tf_op jit(solution)/shard_map/ppermute | solution.py:21
  210.9 4.3 %collective-permute-start.8 = (bf16[32,1,512]{2,1,0:T(2,128)(2,1)S(1)}, bf16[32,1,512]{2,1,0:T(2,128)(2,1)S(1)}, u32[]{:S(2)}, u32[]{:S(2)}) collective-permute-start(bf16[32,1,512]{2,1,0:T(2,128)(2,1)S(1)} %get-tuple-element.23), channel_id=1, source_target_pairs={{1,0},{2,1},{3,2},{4,3},{5,4},{6,5},{7,6},{8,7},{9,8},{10,9},{11,1... | collective-permute-start | bytes 98312 | tf_op jit(solution)/shard_map/ppermute | solution.py:23
  212.2 3.9 %collective-permute-start.9 = (bf16[32,1,512]{2,1,0:T(2,128)(2,1)S(1)}, bf16[32,1,512]{2,1,0:T(2,128)(2,1)S(1)}, u32[]{:S(2)}, u32[]{:S(2)}) collective-permute-start(bf16[32,1,512]{2,1,0:T(2,128)(2,1)S(1)} %get-tuple-element.22), channel_id=1, source_target_pairs={{0,1},{1,2},{2,3},{3,4},{4,5},{5,6},{6,7},{7,8},{8,9},{9,10},{10,1... | collective-permute-start | bytes 98312 | tf_op jit(solution)/shard_map/ppermute | solution.py:21
  219.7 4.6 %collective-permute-start.13 = (bf16[32,16,512]{2,1,0:T(8,128)(2,1)S(1)}, bf16[32,16,512]{2,1,0:T(8,128)(2,1)S(1)}, u32[]{:S(2)}, u32[]{:S(2)}) collective-permute-start(bf16[32,16,512]{2,1,0:T(8,128)(2,1)S(1)} %get-tuple-element.18), channel_id=1, source_target_pairs={{1,0},{2,1},{3,2},{4,3},{5,4},{6,5},{7,6},{8,7},{9,8},{10,9},{11,1... | collective-permute-start | bytes 1572872 | tf_op jit(solution)/shard_map/ppermute | solution.py:23
  221.0 4.6 %collective-permute-start.12 = (bf16[32,16,512]{2,1,0:T(8,128)(2,1)S(1)}, bf16[32,16,512]{2,1,0:T(8,128)(2,1)S(1)}, u32[]{:S(2)}, u32[]{:S(2)}) collective-permute-start(bf16[32,16,512]{2,1,0:T(8,128)(2,1)S(1)} %get-tuple-element.18), channel_id=1, source_target_pairs={{0,1},{1,2},{2,3},{3,4},{4,5},{5,6},{6,7},{7,8},{8,9},{9,10},{10,1... | collective-permute-start | bytes 1572872 | tf_op jit(solution)/shard_map/ppermute | solution.py:21
  246.4 11.2 %copy-start.2 = (bf16[32,16,512]{2,1,0:T(8,128)(2,1)S(1)}, bf16[32,16,512]{2,1,0:T(8,128)(2,1)}, u32[]{:S(2)}) copy-start(bf16[32,16,512]{2,1,0:T(8,128)(2,1)} %get-tuple-element.8) | copy-start | bytes 1572868
  246.5 21.4 %copy-start.5 = (f32[32,16,512]{2,1,0:T(8,128)S(1)}, f32[32,16,512]{2,1,0:T(8,128)}, u32[]{:S(2)}) copy-start(f32[32,16,512]{2,1,0:T(8,128)} %get-tuple-element.9) | copy-start | bytes 3145732
  246.5 21.4 %collective-permute-start.15 = (bf16[32,16,512]{2,1,0:T(8,128)(2,1)S(1)}, bf16[32,16,512]{2,1,0:T(8,128)(2,1)S(1)}, u32[]{:S(2)}, u32[]{:S(2)}) collective-permute-start(bf16[32,16,512]{2,1,0:T(8,128)(2,1)S(1)} %get-tuple-element.15), channel_id=1, source_target_pairs={{1,0},{2,1},{3,2},{4,3},{5,4},{6,5},{7,6},{8,7},{9,8},{10,9},{11,1... | collective-permute-start | bytes 1572872 | tf_op jit(solution)/shard_map/ppermute | solution.py:33
  247.9 20.0 %collective-permute-start.14 = (bf16[32,16,512]{2,1,0:T(8,128)(2,1)S(1)}, bf16[32,16,512]{2,1,0:T(8,128)(2,1)S(1)}, u32[]{:S(2)}, u32[]{:S(2)}) collective-permute-start(bf16[32,16,512]{2,1,0:T(8,128)(2,1)S(1)} %get-tuple-element.14), channel_id=1, source_target_pairs={{0,1},{1,2},{2,3},{3,4},{4,5},{5,6},{6,7},{7,8},{8,9},{9,10},{10,1... | collective-permute-start | bytes 1572872 | tf_op jit(solution)/shard_map/ppermute | solution.py:33
  257.8 9.1 %collective-permute-start.10 = (bf16[32,1,512]{2,1,0:T(2,128)(2,1)S(1)}, bf16[32,1,512]{2,1,0:T(2,128)(2,1)S(1)}, u32[]{:S(2)}, u32[]{:S(2)}) collective-permute-start(bf16[32,1,512]{2,1,0:T(2,128)(2,1)S(1)} %get-tuple-element.21), channel_id=1, source_target_pairs={{1,0},{2,1},{3,2},{4,3},{5,4},{6,5},{7,6},{8,7},{9,8},{10,9},{11,1... | collective-permute-start | bytes 98312 | tf_op jit(solution)/shard_map/ppermute | solution.py:23
  259.1 7.8 %collective-permute-start.11 = (bf16[32,1,512]{2,1,0:T(2,128)(2,1)S(1)}, bf16[32,1,512]{2,1,0:T(2,128)(2,1)S(1)}, u32[]{:S(2)}, u32[]{:S(2)}) collective-permute-start(bf16[32,1,512]{2,1,0:T(2,128)(2,1)S(1)} %get-tuple-element.20), channel_id=1, source_target_pairs={{0,1},{1,2},{2,3},{3,4},{4,5},{5,6},{6,7},{7,8},{8,9},{9,10},{10,1... | collective-permute-start | bytes 98312 | tf_op jit(solution)/shard_map/ppermute | solution.py:21
  339.9 2.0 copy-start.3
where the time goes:
time: 351 us; the launch traced here: 347 us
  blocking collectives  182 us (52%)
  starting transfers between devices  61.8 us (18%)
  matrix products  58.5 us (17%)
  other arithmetic  37.1 us (11%)
    psum x1, blocking collectives, body(): res_gram = lax.psum(gram_matrix(residual, residual), 'row')  62.1 us
    psum x1, blocking collectives, body(): dir_gram = lax.psum(gram_matrix(direction, image), 'row')  61.6 us
    psum x1, blocking collectives, body(): new_gram = lax.psum(gram_matrix(residual, residual), 'row')  57.9 us
    ppermute x4, starting transfers between devices, shifted(): return lax.ppermute(block, axis, route)  27 us
    ppermute x6, starting transfers between devices, extended_2(): lax.ppermute(tail, axis, [(i, (i + 1) % count) for i in range(ends)])  26.9 us
    dot_general x2, matrix products, body(): jnp.einsum('kto,tfoc->ktfc', scaled, weights, preferred_element_type=jnp....  23.9 us
    dot_general x2, matrix products, body(): jnp.einsum('kjc,jr->krc', adjoint, selector, precision=lax.Precision.HIGH...  13.2 us
    another operation x9, other arithmetic, solve_small(): factor = jnp.linalg.cholesky(0.5 * (matrix + matrix.T))  10.8 us
  transfers between devices with their start and end apart: 16, of which 3 were waited for; matrix products, arithmetic and copies ran while one was open for 2% of the time, Pallas kernels for 0%

commit v1 on v0

v1 whole, which is shorter than its diff:
```python
import functools

import jax
import jax.numpy as jnp
from jax import lax
from jax.experimental import pallas as pl
from jax.experimental.pallas import tpu as pltpu
from jax.sharding import PartitionSpec as P

RADIX = 4
HIGHEST = lax.Precision.HIGHEST
NN = (((1,), (0,)), ((), ()))
NT = (((1,), (1,)), ((), ()))
FIELD_EDGE, HALO, INNER_EDGE, TERMS = range(4)


def radices(n):
    out, stride = [], 1
    while stride < n:
        radix = RADIX if (n // stride) % RADIX == 0 else n // stride
        out.append((stride, radix))
        stride *= radix
    return out


def dot(a, b, dims=NN, precision=HIGHEST):
    return lax.dot_general(a, b, dims, precision=precision, preferred_element_type=jnp.float32)


def eliminate(mats):
    k = mats[0].shape[0]
    row_id = lax.broadcasted_iota(jnp.int32, mats[0].shape, 0)
    for i in range(k):
        new = []
        for a in mats:
            row = a[i : i + 1, :] * (1.0 / a[i : i + 1, i : i + 1])
            new.append(jnp.where(row_id == i, row, a - a[:, i : i + 1] * row))
        mats = new
    return mats


def kernel(
    n,
    rhs_ref, kap_ref, inv_ref, mask_ref, w_hbm, prec_ref, idx_ref,
    sol_ref, res_ref,
    w, ext, adj, sc, masked, img, image2, dirn, es, er, ts, tr, ar, aug,
    wsem, send_sem, recv_sem, ar_send, ar_recv,
):
    rows, nk, cols = rhs_ref.shape
    tiles, foot, obs, _ = w.shape
    picks = tiles * foot
    me = lax.axis_index("row")
    has_up, has_down = me > 0, me < n - 1
    levels = radices(n)

    for t in range(tiles):
        pltpu.make_async_copy(w_hbm.at[t], w.at[t], wsem.at[t]).start()

    def neighbour(d):
        return {"row": lax.rem(me + (1 if d == 0 else n - 1), n)}

    def partner(stride, radix, d):
        q = lax.rem(me // stride, radix)
        return {"row": me + (lax.rem(q + d, radix) - q) * stride}

    barrier = pltpu.get_barrier_semaphore()

    def greet(device):
        pl.semaphore_signal(barrier, inc=1, device_id=device, device_id_type=pl.DeviceIdType.MESH)

    count = 0
    for stride, radix in levels:
        for d in range(1, radix):
            greet(partner(stride, radix, d))
            count += 1
    pl.when(has_down)(lambda: greet(neighbour(0)))
    pl.when(has_up)(lambda: greet(neighbour(1)))

    def copy(it, kind, d, src, dst):
        return pltpu.make_async_remote_copy(
            src_ref=src,
            dst_ref=dst,
            send_sem=send_sem.at[it, kind, d],
            recv_sem=recv_sem.at[it, kind, d],
            device_id=neighbour(d),
            device_id_type=pl.DeviceIdType.MESH,
        )

    sends = (has_down, has_up)
    receives = (has_up, has_down)

    def pair(it, kind):
        if kind == HALO:
            own = ext.at[it, pl.ds(rows, rows)]
            return (
                copy(it, kind, 0, own, ext.at[it, pl.ds(0, rows)]),
                copy(it, kind, 1, own, ext.at[it, pl.ds(2 * rows, rows)]),
            )
        if kind == TERMS:
            return tuple(copy(it, kind, d, ts.at[it, d], tr.at[it, d]) for d in range(2))
        e = 0 if kind == FIELD_EDGE else 1
        return tuple(copy(it, kind, d, es.at[it, e, d], er.at[it, e, d]) for d in range(2))

    def start(it, kind):
        for d, c in enumerate(pair(it, kind)):
            pl.when(sends[d])(c.start)

    def arrive(it, kind):
        for d, c in enumerate(pair(it, kind)):
            pl.when(receives[d])(c.wait_recv)

    def drain(it, kind):
        for d, c in enumerate(pair(it, kind)):
            pl.when(sends[d])(c.wait_send)

    @pl.when(jnp.logical_not(has_up))
    def _():
        for it in range(2):
            ext[it, pl.ds(0, rows)] = jnp.zeros((rows, nk, cols), jnp.bfloat16)
            tr[it, 0] = jnp.zeros((rows, nk, cols), jnp.bfloat16)
            for e in range(2):
                er[it, e, 0] = jnp.zeros((nk, cols), jnp.bfloat16)

    @pl.when(jnp.logical_not(has_down))
    def _():
        for it in range(2):
            ext[it, pl.ds(2 * rows, rows)] = jnp.zeros((rows, nk, cols), jnp.bfloat16)
            tr[it, 1] = jnp.zeros((rows, nk, cols), jnp.bfloat16)
            for e in range(2):
                er[it, e, 1] = jnp.zeros((nk, cols), jnp.bfloat16)

    adj[0] = jnp.zeros((nk, cols), jnp.float32)

    lane = lax.broadcasted_iota(jnp.int32, (nk, cols), 1)
    maskf = mask_ref[...].astype(jnp.float32)
    kap = kap_ref[...]
    inv = inv_ref[...]

    def at(table, r):
        return table[r : r + 1, :]

    def beside(r):
        m = masked[r + 1]
        right = jnp.where(lane == cols - 1, 0.0, pltpu.roll(m, cols - 1, 1))
        left = jnp.where(lane == 0, 0.0, pltpu.roll(m, 1, 1))
        return masked[r] + masked[r + 2] + right + left

    def stage_edges(it, e):
        for d, r in ((0, rows), (1, 1)):
            es[it, e, d] = masked[r].astype(jnp.bfloat16)

    def take_edges(it, e):
        masked[0] = er[it, e, 0].astype(jnp.float32)
        masked[rows + 1] = er[it, e, 1].astype(jnp.float32)

    def apply(it, field, out):
        for r in range(rows):
            masked[r + 1] = at(maskf, r) * field[r]
            ext[it, rows + r] = field[r].astype(jnp.bfloat16)
        stage_edges(it, 0)
        if it == 0:
            down, up = (jnp.where(x, 1, 0) for x in (has_down, has_up))
            pl.semaphore_wait(barrier, count + down + up)
        start(it, FIELD_EDGE)
        start(it, HALO)
        arrive(it, FIELD_EDGE)
        take_edges(it, 0)
        for r in range(rows):
            out[r] = at(kap, r) * field[r] + at(maskf, r) * (4.0 * field[r] - beside(r))
        for r in range(rows):
            out[r] = at(inv, r) * out[r]
            masked[r + 1] = at(maskf, r) * out[r]
        stage_edges(it, 1)
        start(it, INNER_EDGE)
        arrive(it, HALO)

        def observe(t, carry):
            if it == 0:
                pltpu.make_async_copy(w_hbm.at[t], w.at[t], wsem.at[t]).wait()
            total = jnp.zeros((nk, obs), jnp.float32)
            for j in range(foot):
                x = ext[it, idx_ref[t * foot + j]]
                total += dot(x, w[t, j], NT, None)
            sc[t] = (prec_ref[pl.ds(t, 1), :] * total).astype(jnp.bfloat16)
            return carry

        lax.fori_loop(0, tiles, observe, 0)

        def spread(t, carry):
            for j in range(foot):
                adj[1 + t * foot + j] = dot(sc[t], w[t, j], NN, None)
            return carry

        lax.fori_loop(0, tiles, spread, 0)

        def link(i, carry):
            adj[1 + i] = adj[1 + i] + adj[idx_ref[picks + i]]
            return carry

        lax.fori_loop(0, picks, link, 0)

        def stage(r, carry):
            ts[it, 1, r] = adj[idx_ref[2 * picks + r]].astype(jnp.bfloat16)
            ts[it, 0, r] = adj[idx_ref[2 * picks + 2 * rows + r]].astype(jnp.bfloat16)
            return carry

        lax.fori_loop(0, rows, stage, 0)
        start(it, TERMS)
        arrive(it, INNER_EDGE)
        take_edges(it, 1)
        for r in range(rows):
            prior = at(kap, r) * out[r] + at(maskf, r) * (4.0 * out[r] - beside(r))
            out[r] = prior + adj[idx_ref[2 * picks + rows + r]]
        arrive(it, TERMS)
        for r in range(rows):
            out[r] += tr[it, 0, r].astype(jnp.float32) + tr[it, 1, r].astype(jnp.float32)
        for kind in range(4):
            drain(it, kind)

    def grams(a, b):
        parts = [jnp.zeros((nk, nk), jnp.float32) for _ in range(4)]
        for r in range(rows):
            x, y = a[r], b[r]
            for p, (f, g) in enumerate(((x, x), (x, y), (y, x), (y, y))):
                parts[p] += dot(f, g, NT)
        return parts

    def reduce_all(which, parts):
        value = jnp.concatenate(parts, axis=1)
        for lv, (stride, radix) in enumerate(levels):
            q = lax.rem(me // stride, radix)
            ar[which, lv, q] = value
            copies = [
                pltpu.make_async_remote_copy(
                    src_ref=ar.at[which, lv, q],
                    dst_ref=ar.at[which, lv, q],
                    send_sem=ar_send.at[which, lv, d],
                    recv_sem=ar_recv.at[which, lv, d],
                    device_id=partner(stride, radix, d),
                    device_id_type=pl.DeviceIdType.MESH,
                )
                for d in range(1, radix)
            ]
            for c in copies:
                c.start()
            for c in copies:
                c.wait_recv()
            for c in copies:
                c.wait_send()
            value = ar[which, lv, 0]
            for p in range(1, radix):
                value = value + ar[which, lv, p]
        return [value[:, p * nk : (p + 1) * nk] for p in range(4)]

    eye = (
        lax.broadcasted_iota(jnp.int32, (nk, nk), 0) == lax.broadcasted_iota(jnp.int32, (nk, nk), 1)
    ).astype(jnp.float32)
    pad = jnp.zeros((nk, 2 * nk), jnp.float32)

    def flipped(x):
        return dot(eye, x, NT)

    apply(0, rhs_ref, img)
    g00, g01, g10, g11 = reduce_all(0, grams(rhs_ref, img))
    first, second = eliminate(
        [
            jnp.concatenate([0.5 * (g01 + g10), g00, pad], axis=1),
            jnp.concatenate([g00, eye, pad], axis=1),
        ]
    )
    step = first[:, nk : 2 * nk]
    step_t = flipped(step)
    cross = dot(g01, step)
    new_gram = g00 - cross - flipped(cross) + dot(step_t, dot(g11, step))
    mix = dot(second[:, nk : 2 * nk], new_gram)
    mix_t = flipped(mix)
    for r in range(rows):
        b = rhs_ref[r]
        both = dot(jnp.concatenate([step_t, mix_t], axis=0), b)
        left = b - dot(step_t, img[r])
        sol_ref[r] = both[:nk]
        res_ref[r] = left
        dirn[r] = left + both[nk:]

    apply(1, dirn, image2)
    _, g01, g10, _ = reduce_all(1, grams(dirn, image2))
    (third,) = eliminate([jnp.concatenate([0.5 * (g01 + g10), new_gram, pad], axis=1)])
    step_t = flipped(third[:, nk : 2 * nk])
    for r in range(rows):
        sol_ref[r] += dot(step_t, dirn[r])
        res_ref[r] -= dot(step_t, image2[r])


def body(right_sides, kappa_sq, inv_mass, cell_mask, weights, obs_precision, footprint):
    nk, rows, cols = right_sides.shape
    tiles, foot, obs, _ = weights.shape
    picks = tiles * foot
    n = lax.axis_size("row")
    device = lax.axis_index("row")
    ids = (footprint - (device * rows - rows)).reshape(-1)
    wanted = jnp.concatenate([ids, jnp.arange(3 * rows, dtype=jnp.int32)])
    before = jnp.concatenate(
        [jnp.arange(picks, dtype=jnp.int32), jnp.full((3 * rows,), picks, jnp.int32)]
    )
    order = jnp.arange(picks, dtype=jnp.int32)
    same = (wanted[:, None] == ids[None, :]) & (order[None, :] < before[:, None])
    last = jnp.max(jnp.where(same, order[None, :] + 1, 0), axis=1)
    index = jnp.concatenate([ids, last])

    levels = len(radices(n))
    field = (rows, nk, cols)
    vmem = pl.BlockSpec(memory_space=pltpu.VMEM)
    f32, bf16 = jnp.float32, jnp.bfloat16
    solved, left = pl.pallas_call(
        functools.partial(kernel, n),
        out_shape=[jax.ShapeDtypeStruct(field, f32)] * 2,
        in_specs=[vmem] * 4
        + [pl.BlockSpec(memory_space=pl.ANY), vmem, pl.BlockSpec(memory_space=pltpu.SMEM)],
        out_specs=[vmem] * 2,
        scratch_shapes=[
            pltpu.VMEM(weights.shape, bf16),
            pltpu.VMEM((2, 3 * rows, nk, cols), bf16),
            pltpu.VMEM((picks + 1, nk, cols), f32),
            pltpu.VMEM((tiles, nk, obs), bf16),
            pltpu.VMEM((rows + 2, nk, cols), f32),
            pltpu.VMEM(field, f32),
            pltpu.VMEM(field, f32),
            pltpu.VMEM(field, f32),
            pltpu.VMEM((2, 2, 2, nk, cols), bf16),
            pltpu.VMEM((2, 2, 2, nk, cols), bf16),
            pltpu.VMEM((2, 2) + field, bf16),
            pltpu.VMEM((2, 2) + field, bf16),
            pltpu.VMEM((2, levels, RADIX, nk, 4 * nk), f32),
            pltpu.VMEM((2, nk, 4 * nk), f32),
            pltpu.SemaphoreType.DMA((tiles,)),
            pltpu.SemaphoreType.DMA((2, 4, 2)),
            pltpu.SemaphoreType.DMA((2, 4, 2)),
            pltpu.SemaphoreType.DMA((2, levels, RADIX)),
            pltpu.SemaphoreType.DMA((2, levels, RADIX)),
        ],
        compiler_params=pltpu.CompilerParams(
            collective_id=0, has_side_effects=True, vmem_limit_bytes=50 * 1024 * 1024
        ),
    )(
        jnp.swapaxes(right_sides, 0, 1),
        kappa_sq,
        inv_mass,
        cell_mask,
        weights,
        obs_precision,
        index,
    )
    return (jnp.swapaxes(solved, 0, 1), jnp.swapaxes(left, 0, 1))


def solution(mesh):
    placed = (
        P(None, ("grp", "row"), None),
        P(("grp", "row"), None),
        P(("grp", "row"), None),
        P(("grp", "row"), None),
        P(("grp", "row"), None, None, None),
        P(("grp", "row"), None),
        P(("grp", "row"), None),
    )
    return jax.shard_map(
        body,
        mesh=mesh,
        in_specs=placed,
        out_specs=(P(None, ("grp", "row"), None), P(None, ("grp", "row"), None)),
        check_vma=False,
    )
```

time: 351 us -> 105 us (0.30); the launches traced: 347 us -> 105 us
  blocking collectives: 182 us -> 0 us
  Pallas kernels: 0 us -> 94.3 us
  starting transfers between devices: 61.8 us -> 0 us
  matrix products: 58.5 us -> 0 us
  other arithmetic: 37.1 us -> 1.6 us
  local copies, waits for them, and re-layouts: 3.49 us -> 8.04 us
    psum x3 -> x0, blocking collectives: 182 us -> none  [the longest x1 62.1 us: body(): res_gram = lax.psum(gram_matrix(residual, residual), 'row')]
    pallas_call x0 -> x1, Pallas kernels: none -> 94.3 us  [body(): pl.pallas_call(functools.partial(kernel, n), out_shape=[jax.ShapeDtypeStr...]
    ppermute x16 -> x0, starting transfers between devices: 61.8 us -> none  [the longest x4 27 us: shifted(): return lax.ppermute(block, axis, route)]
    dot_general x15 -> x0, matrix products: 57.2 us -> none  [the longest x2 23.9 us: body(): jnp.einsum('kto,tfoc->ktfc', scaled, weights, preferred_element_type=jnp....]
    another operation x15 -> x0, other arithmetic: 20 us -> none  [the longest x9 10.8 us: solve_small(): factor = jnp.linalg.cholesky(0.5 * (matrix + matrix.T))]
    convert_element_type x5 -> x0, other arithmetic: 7.77 us -> none  [the longest x4 6.93 us: shortened(): a.astype(jnp.bfloat16)]
    unnamed x25 -> x11, local copies, waits for them, and re-layouts: 2.42 us -> 7.96 us
    concatenate x4 -> x2, other arithmetic: 4.24 us -> 0.15 us  [the longest x1 0.08 us: body(): wanted = jnp.concatenate([ids, jnp.arange(3 * rows, dtype=jnp.int32)])]
  transfers between devices with their start and end apart: 16 -> 0, of which waited for: 3 -> 0; matrix products, arithmetic and copies ran while one was open for 2% -> 0% of each run, Pallas kernels for 0% -> 0%
where the time goes in v1:
time: 105 us
  Pallas kernels  94.3 us (90%)
  local copies, waits for them, and re-layouts  8.04 us (8%)
  other arithmetic  1.6 us (2%)
    pallas_call x1, Pallas kernels, body(): pl.pallas_call(functools.partial(kernel, n), out_shape=[jax.ShapeDtypeStr...  94.3 us
    unnamed x11, local copies, waits for them, and re-layouts  7.96 us

profile of v1, /device:TPU:0, one launch (start us, length us, event | category | flops | bytes accessed | tf_op | source)
XLA Modules:
  0.0 104.7 jit_solution(7811420665012244924)
XLA Ops:
  0.7 0.7 broadcast_subtract_fusion
  1.3 0.1 reshape.15
  1.4 0.1 pad_add_fusion.1
  1.5 0.8 select_reduce_fusion
  2.3 0.1 pad_add_fusion.idx_ref
  2.3 1.8 %copy.16 = f32[32,16,512]{2,0,1:T(8,128)S(1)} copy(f32[32,16,512]{2,1,0:T(8,128)} %param.7) | data formatting | bytes 2097152 | tf_op args[0]
  4.2 0.0 copy-start
  4.2 0.7 copy-done
  4.9 0.0 copy-start.1
  4.9 0.8 copy-done.1
  5.7 0.0 copy-start.2
  5.7 0.8 copy-done.2
  6.5 0.0 copy-start.3
  6.5 0.7 copy-done.3
  7.1 94.3 %shard_map.86 = (f32[16,32,512]{2,1,0:T(8,128)S(1)}, f32[16,32,512]{2,1,0:T(8,128)S(1)}) custom-call(f32[16,32,512]{2,1,0:T(8,128)S(1)} %bitcast.5, f32[16,512]{1,0:T(8,128)S(1)} %copy-done, f32[16,512]{1,0:T(8,128)S(1)} %copy-done.1, s32[16,512]{1,0:T(8,128)S(1)} %copy-done.2, bf16[8,8,128,512]{3,2,1,0:T(8,128)(2,1)} %w_hbm.1, f32[8,128]{1,0:T(8,128)S(1)} %copy-done.3, ...), custom_call_target="tpu_custom_call" | custom-call | tf_op jit(solution)/shard_map/pallas_call | solution.py:314
  101.5 1.6 %copy.13 = f32[32,16,512]{2,1,0:T(8,128)} copy(f32[32,16,512]{2,0,1:T(8,128)S(1)} %bitcast.7) | data formatting | bytes 2097152
  103.1 1.6 %copy.14 = f32[32,16,512]{2,1,0:T(8,128)} copy(f32[32,16,512]{2,0,1:T(8,128)S(1)} %bitcast.6) | data formatting | bytes 2097152
  (2 shorter events, 0.0 us)
Async XLA Ops:
  4.2 0.8 copy-start
  4.9 0.8 copy-start.1
  5.7 0.8 copy-start.2
  6.5 0.7 copy-start.3

commit v2 on v1

--- a/solution.py
+++ b/solution.py
@@ -7,17 +7,19 @@
 from jax.experimental.pallas import tpu as pltpu
 from jax.sharding import PartitionSpec as P
 
-RADIX = 4
+RADIX = 16
+HALVES = 2
 HIGHEST = lax.Precision.HIGHEST
 NN = (((1,), (0,)), ((), ()))
 NT = (((1,), (1,)), ((), ()))
 FIELD_EDGE, HALO, INNER_EDGE, TERMS = range(4)
+KINDS = TERMS + HALVES
 
 
 def radices(n):
     out, stride = [], 1
     while stride < n:
-        radix = RADIX if (n // stride) % RADIX == 0 else n // stride
+        radix = min(RADIX, n // stride)
         out.append((stride, radix))
         stride *= radix
     return out
@@ -41,10 +43,10 @@
 
 def kernel(
     n,
-    rhs_ref, kap_ref, inv_ref, mask_ref, w_hbm, prec_ref, idx_ref,
+    rhs_ref, kap_hbm, inv_hbm, mask_hbm, w_hbm, prec_hbm, idx_ref,
     sol_ref, res_ref,
-    w, ext, adj, sc, masked, img, image2, dirn, es, er, ts, tr, ar, aug,
-    wsem, send_sem, recv_sem, ar_send, ar_recv,
+    w, ext, adj, sc, masked, img, image2, dirn, es, er, ts, tr, ar0, ar1, packed,
+    kap_ref, inv_ref, mask_ref, prec_ref, tsem, wsem, send_sem, recv_sem, ar_send, ar_recv,
 ):
     rows, nk, cols = rhs_ref.shape
     tiles, foot, obs, _ = w.shape
@@ -53,6 +55,15 @@
     has_up, has_down = me > 0, me < n - 1
     levels = radices(n)
 
+    half = cols // HALVES
+    tables = [
+        pltpu.make_async_copy(src, dst, tsem.at[i])
+        for i, (src, dst) in enumerate(
+            ((kap_hbm, kap_ref), (inv_hbm, inv_ref), (mask_hbm, mask_ref), (prec_hbm, prec_ref))
+        )
+    ]
+    for c in tables:
+        c.start()
     for t in range(tiles):
         pltpu.make_async_copy(w_hbm.at[t], w.at[t], wsem.at[t]).start()
 
@@ -96,8 +107,9 @@
                 copy(it, kind, 0, own, ext.at[it, pl.ds(0, rows)]),
                 copy(it, kind, 1, own, ext.at[it, pl.ds(2 * rows, rows)]),
             )
-        if kind == TERMS:
-            return tuple(copy(it, kind, d, ts.at[it, d], tr.at[it, d]) for d in range(2))
+        if kind >= TERMS:
+            h = kind - TERMS
+            return tuple(copy(it, kind, d, ts.at[it, h, d], tr.at[it, h, d]) for d in range(2))
         e = 0 if kind == FIELD_EDGE else 1
         return tuple(copy(it, kind, d, es.at[it, e, d], er.at[it, e, d]) for d in range(2))
 
@@ -117,7 +129,8 @@
     def _():
         for it in range(2):
             ext[it, pl.ds(0, rows)] = jnp.zeros((rows, nk, cols), jnp.bfloat16)
-            tr[it, 0] = jnp.zeros((rows, nk, cols), jnp.bfloat16)
+            for h in range(HALVES):
+                tr[it, h, 0] = jnp.zeros((rows, nk, half), jnp.bfloat16)
             for e in range(2):
                 er[it, e, 0] = jnp.zeros((nk, cols), jnp.bfloat16)
 
@@ -125,11 +138,15 @@
     def _():
         for it in range(2):
             ext[it, pl.ds(2 * rows, rows)] = jnp.zeros((rows, nk, cols), jnp.bfloat16)
-            tr[it, 1] = jnp.zeros((rows, nk, cols), jnp.bfloat16)
+            for h in range(HALVES):
+                tr[it, h, 1] = jnp.zeros((rows, nk, half), jnp.bfloat16)
             for e in range(2):
                 er[it, e, 1] = jnp.zeros((nk, cols), jnp.bfloat16)
 
-    adj[0] = jnp.zeros((nk, cols), jnp.float32)
+    for h in range(HALVES):
+        adj[h, 0] = jnp.zeros((nk, half), jnp.float32)
+    for c in tables:
+        c.wait()
 
     lane = lax.broadcasted_iota(jnp.int32, (nk, cols), 1)
     maskf = mask_ref[...].astype(jnp.float32)
@@ -184,56 +201,77 @@
             sc[t] = (prec_ref[pl.ds(t, 1), :] * total).astype(jnp.bfloat16)
             return carry
 
-        lax.fori_loop(0, tiles, observe, 0)
-
-        def spread(t, carry):
-            for j in range(foot):
-                adj[1 + t * foot + j] = dot(sc[t], w[t, j], NN, None)
-            return carry
-
-        lax.fori_loop(0, tiles, spread, 0)
-
-        def link(i, carry):
-            adj[1 + i] = adj[1 + i] + adj[idx_ref[picks + i]]
-            return carry
-
-        lax.fori_loop(0, picks, link, 0)
-
-        def stage(r, carry):
-            ts[it, 1, r] = adj[idx_ref[2 * picks + r]].astype(jnp.bfloat16)
-            ts[it, 0, r] = adj[idx_ref[2 * picks + 2 * rows + r]].astype(jnp.bfloat16)
-            return carry
-
-        lax.fori_loop(0, rows, stage, 0)
-        start(it, TERMS)
+        lax.fori_loop(0, tiles, observe, 0, unroll=2)
+
+        for h in range(HALVES):
+            part = pl.ds(h * half, half)
+
+            def spread(t, carry):
+                for j in range(foot):
+                    adj[h, 1 + t * foot + j] = dot(sc[t], w[t, j, :, part], NN, None)
+                return carry
+
+            lax.fori_loop(0, tiles, spread, 0, unroll=2)
+
+            def link(i, carry):
+                adj[h, 1 + i] = adj[h, 1 + i] + adj[h, idx_ref[picks + i]]
+                return carry
+
+            lax.fori_loop(0, picks, link, 0, unroll=4)
+
+            def stage(r, carry):
+                ts[it, h, 1, r] = adj[h, idx_ref[2 * picks + r]].astype(jnp.bfloat16)
+                ts[it, h, 0, r] = adj[h, idx_ref[2 * picks + 2 * rows + r]].astype(jnp.bfloat16)
+                return carry
+
+            lax.fori_loop(0, rows, stage, 0, unroll=4)
+            start(it, TERMS + h)
         arrive(it, INNER_EDGE)
         take_edges(it, 1)
         for r in range(rows):
-            prior = at(kap, r) * out[r] + at(maskf, r) * (4.0 * out[r] - beside(r))
-            out[r] = prior + adj[idx_ref[2 * picks + rows + r]]
-        arrive(it, TERMS)
+            out[r] = at(kap, r) * out[r] + at(maskf, r) * (4.0 * out[r] - beside(r))
+        for h in range(HALVES):
+            part = pl.ds(h * half, half)
+            arrive(it, TERMS + h)
+            for r in range(rows):
+                beyond = tr[it, h, 0, r].astype(jnp.float32) + tr[it, h, 1, r].astype(jnp.float32)
+                out[r, :, part] += adj[h, idx_ref[2 * picks + rows + r]] + beyond
+        for kind in range(KINDS):
+            drain(it, kind)
+
+    def halves_of(x):
+        high = x.astype(jnp.bfloat16)
+        return high, (x - high.astype(jnp.float32)).astype(jnp.bfloat16)
+
+    def pack(a, b):
+        total = jnp.zeros((4 * nk, 4 * nk), jnp.float32)
         for r in range(rows):
-            out[r] += tr[it, 0, r].astype(jnp.float32) + tr[it, 1, r].astype(jnp.float32)
-        for kind in range(4):
-            drain(it, kind)
-
-    def grams(a, b):
-        parts = [jnp.zeros((nk, nk), jnp.float32) for _ in range(4)]
-        for r in range(rows):
-            x, y = a[r], b[r]
-            for p, (f, g) in enumerate(((x, x), (x, y), (y, x), (y, y))):
-                parts[p] += dot(f, g, NT)
-        return parts
-
-    def reduce_all(which, parts):
-        value = jnp.concatenate(parts, axis=1)
+            a_high, a_low = halves_of(a[r])
+            b_high, b_low = halves_of(b[r])
+            x = jnp.concatenate([a_high, b_high, a_low, b_low], axis=0)
+            packed[r] = x
+            total += dot(x, x, NT, None)
+        total = total[: 2 * nk] + total[2 * nk :]
+        return total[:, : 2 * nk] + total[:, 2 * nk :]
+
+    def combine(coeffs):
+        high, low = halves_of(coeffs)
+        wide = jnp.concatenate([high, high, low], axis=1)
+
+        def row(r):
+            x = packed[r]
+            return dot(wide, jnp.concatenate([x, x[: 2 * nk]], axis=0), NN, None)
+
+        return row
+
+    def reduce_all(which, ar, value):
         for lv, (stride, radix) in enumerate(levels):
             q = lax.rem(me // stride, radix)
-            ar[which, lv, q] = value
+            ar[lv, q] = value
             copies = [
                 pltpu.make_async_remote_copy(
-                    src_ref=ar.at[which, lv, q],
-                    dst_ref=ar.at[which, lv, q],
+                    src_ref=ar.at[lv, q],
+                    dst_ref=ar.at[lv, q],
                     send_sem=ar_send.at[which, lv, d],
                     recv_sem=ar_recv.at[which, lv, d],
                     device_id=partner(stride, radix, d),
@@ -247,10 +285,10 @@
                 c.wait_recv()
             for c in copies:
                 c.wait_send()
-            value = ar[which, lv, 0]
+            value = ar[lv, 0]
             for p in range(1, radix):
-                value = value + ar[which, lv, p]
-        return [value[:, p * nk : (p + 1) * nk] for p in range(4)]
+                value = value + ar[lv, p]
+        return value
 
     eye = (
         lax.broadcasted_iota(jnp.int32, (nk, nk), 0) == lax.broadcasted_iota(jnp.int32, (nk, nk), 1)
@@ -261,7 +299,9 @@
         return dot(eye, x, NT)
 
     apply(0, rhs_ref, img)
-    g00, g01, g10, g11 = reduce_all(0, grams(rhs_ref, img))
+    total = pack(rhs_ref, img)
+    total = reduce_all(0, ar0, jnp.concatenate([total[:nk], total[nk:]], axis=1))
+    g00, g01, g10, g11 = (total[:, p * nk : (p + 1) * nk] for p in range(4))
     first, second = eliminate(
         [
             jnp.concatenate([0.5 * (g01 + g10), g00, pad], axis=1),
@@ -270,25 +310,48 @@
     )
     step = first[:, nk : 2 * nk]
     step_t = flipped(step)
-    cross = dot(g01, step)
-    new_gram = g00 - cross - flipped(cross) + dot(step_t, dot(g11, step))
-    mix = dot(second[:, nk : 2 * nk], new_gram)
-    mix_t = flipped(mix)
+    new_gram = g00 - dot(g01, step) - dot(step_t, g10 - dot(g11, step))
+    mix_t = dot(new_gram, second[:, nk : 2 * nk])
+    none = jnp.zeros((nk, nk), jnp.float32)
+    rows_of = combine(
+        jnp.concatenate(
+            [
+                jnp.concatenate([step_t, none], axis=1),
+                jnp.concatenate([none, step_t], axis=1),
+                jnp.concatenate([mix_t, none], axis=1),
+            ],
+            axis=0,
+        )
+    )
     for r in range(rows):
-        b = rhs_ref[r]
-        both = dot(jnp.concatenate([step_t, mix_t], axis=0), b)
-        left = b - dot(step_t, img[r])
-        sol_ref[r] = both[:nk]
+        all_three = rows_of(r)
+        left = rhs_ref[r] - all_three[nk : 2 * nk]
+        sol_ref[r] = all_three[:nk]
         res_ref[r] = left
-        dirn[r] = left + both[nk:]
+        dirn[r] = left + all_three[2 * nk :]
 
     apply(1, dirn, image2)
-    _, g01, g10, _ = reduce_all(1, grams(dirn, image2))
-    (third,) = eliminate([jnp.concatenate([0.5 * (g01 + g10), new_gram, pad], axis=1)])
+    total = pack(dirn, image2)
+    total = 0.5 * (total[:nk, nk:] + total[nk:, :nk])
+    fold = nk // 4
+    total = jnp.concatenate([total[p * fold : (p + 1) * fold] for p in range(4)], axis=1)
+    total = reduce_all(1, ar1, total)
+    total = jnp.concatenate([total[:, p * nk : (p + 1) * nk] for p in range(4)], axis=0)
+    (third,) = eliminate([jnp.concatenate([total, new_gram, pad], axis=1)])
     step_t = flipped(third[:, nk : 2 * nk])
+    rows_of = combine(
+        jnp.concatenate(
+            [
+                jnp.concatenate([step_t, none], axis=1),
+                jnp.concatenate([none, step_t], axis=1),
+            ],
+            axis=0,
+        )
+    )
     for r in range(rows):
-        sol_ref[r] += dot(step_t, dirn[r])
-        res_ref[r] -= dot(step_t, image2[r])
+        both = rows_of(r)
+        sol_ref[r] += both[:nk]
+        res_ref[r] -= both[nk:]
 
 
 def body(right_sides, kappa_sq, inv_mass, cell_mask, weights, obs_precision, footprint):
@@ -308,19 +371,21 @@
     index = jnp.concatenate([ids, last])
 
     levels = len(radices(n))
+    half = cols // HALVES
     field = (rows, nk, cols)
     vmem = pl.BlockSpec(memory_space=pltpu.VMEM)
     f32, bf16 = jnp.float32, jnp.bfloat16
     solved, left = pl.pallas_call(
         functools.partial(kernel, n),
         out_shape=[jax.ShapeDtypeStruct(field, f32)] * 2,
-        in_specs=[vmem] * 4
-        + [pl.BlockSpec(memory_space=pl.ANY), vmem, pl.BlockSpec(memory_space=pltpu.SMEM)],
+        in_specs=[vmem]
+        + [pl.BlockSpec(memory_space=pl.ANY)] * 5
+        + [pl.BlockSpec(memory_space=pltpu.SMEM)],
         out_specs=[vmem] * 2,
         scratch_shapes=[
             pltpu.VMEM(weights.shape, bf16),
             pltpu.VMEM((2, 3 * rows, nk, cols), bf16),
-            pltpu.VMEM((picks + 1, nk, cols), f32),
+            pltpu.VMEM((HALVES, picks + 1, nk, half), f32),
             pltpu.VMEM((tiles, nk, obs), bf16),
             pltpu.VMEM((rows + 2, nk, cols), f32),
             pltpu.VMEM(field, f32),
@@ -328,18 +393,24 @@
             pltpu.VMEM(field, f32),
             pltpu.VMEM((2, 2, 2, nk, cols), bf16),
             pltpu.VMEM((2, 2, 2, nk, cols), bf16),
-            pltpu.VMEM((2, 2) + field, bf16),
-            pltpu.VMEM((2, 2) + field, bf16),
-            pltpu.VMEM((2, levels, RADIX, nk, 4 * nk), f32),
-            pltpu.VMEM((2, nk, 4 * nk), f32),
+            pltpu.VMEM((2, HALVES, 2, rows, nk, half), bf16),
+            pltpu.VMEM((2, HALVES, 2, rows, nk, half), bf16),
+            pltpu.VMEM((levels, RADIX, nk, 4 * nk), f32),
+            pltpu.VMEM((levels, RADIX, nk // 4, 4 * nk), f32),
+            pltpu.VMEM((rows, 4 * nk, cols), bf16),
+            pltpu.VMEM(kappa_sq.shape, f32),
+            pltpu.VMEM(inv_mass.shape, f32),
+            pltpu.VMEM(cell_mask.shape, jnp.int32),
+            pltpu.VMEM(obs_precision.shape, f32),
+            pltpu.SemaphoreType.DMA((4,)),
             pltpu.SemaphoreType.DMA((tiles,)),
-            pltpu.SemaphoreType.DMA((2, 4, 2)),
-            pltpu.SemaphoreType.DMA((2, 4, 2)),
+            pltpu.SemaphoreType.DMA((2, KINDS, 2)),
+            pltpu.SemaphoreType.DMA((2, KINDS, 2)),
             pltpu.SemaphoreType.DMA((2, levels, RADIX)),
             pltpu.SemaphoreType.DMA((2, levels, RADIX)),
         ],
         compiler_params=pltpu.CompilerParams(
-            collective_id=0, has_side_effects=True, vmem_limit_bytes=50 * 1024 * 1024
+            collective_id=0, has_side_effects=True, vmem_limit_bytes=60 * 1024 * 1024
         ),
     )(
         jnp.swapaxes(right_sides, 0, 1),

time: 105 us -> 99.6 us (0.949)
  Pallas kernels: 94.3 us -> 88 us
    pallas_call x1, Pallas kernels: 94.3 us -> 88 us  [body(): pl.pallas_call(functools.partial(kernel, n), out_shape=[jax.ShapeDtypeStr...]
    unnamed x11 -> x3, local copies, waits for them, and re-layouts: 7.96 us -> 8.41 us
where the time goes in v2:
time: 99.6 us; the launch traced here: 99.3 us
  Pallas kernels  88 us (88%)
  local copies, waits for them, and re-layouts  8.5 us (9%)
  other arithmetic  2.17 us (2%)
    pallas_call x1, Pallas kernels, body(): pl.pallas_call(functools.partial(kernel, n), out_shape=[jax.ShapeDtypeStr...  88 us
    unnamed x3, local copies, waits for them, and re-layouts  8.41 us

profile of v2, /device:TPU:0, one launch (start us, length us, event | category | flops | bytes accessed | tf_op | source)
XLA Modules:
  0.0 99.3 jit_solution(16613744967129226171)
XLA Ops:
  0.7 0.7 broadcast_subtract_fusion
  1.3 0.1 reshape.15
  1.4 0.1 pad_add_fusion.1
  1.5 0.8 select_reduce_fusion
  2.3 0.6 pad_add_fusion.idx_ref
  2.9 2.8 %copy.16 = f32[32,16,512]{2,0,1:T(8,128)} copy(f32[32,16,512]{2,1,0:T(8,128)} %param.7) | data formatting | bytes 2097152 | tf_op args[0]
  5.7 88.0 %shard_map.86 = (f32[16,32,512]{2,1,0:T(8,128)}, f32[16,32,512]{2,1,0:T(8,128)}) custom-call(f32[16,32,512]{2,1,0:T(8,128)} %bitcast.5, f32[16,512]{1,0:T(8,128)} %kap_hbm.1, f32[16,512]{1,0:T(8,128)} %inv_hbm.1, s32[16,512]{1,0:T(8,128)} %mask_hbm.1, bf16[8,8,128,512]{3,2,1,0:T(8,128)(2,1)} %w_hbm.1, f32[8,128]{1,0:T(8,128)} %prec_hbm.1, ...), custom_call_target="tpu_custom_call" | custom-call | tf_op jit(solution)/shard_map/pallas_call | solution.py:378
  93.7 2.8 %copy.13 = f32[32,16,512]{2,1,0:T(8,128)} copy(f32[32,16,512]{2,0,1:T(8,128)} %bitcast.7) | data formatting | bytes 2097152
  96.5 2.8 %copy.14 = f32[32,16,512]{2,1,0:T(8,128)} copy(f32[32,16,512]{2,0,1:T(8,128)} %bitcast.6) | data formatting | bytes 2097152
  (2 shorter events, 0.0 us)

commit v3 on v2

--- a/solution.py
+++ b/solution.py
@@ -45,7 +45,7 @@
     n,
     rhs_ref, kap_hbm, inv_hbm, mask_hbm, w_hbm, prec_hbm, idx_ref,
     sol_ref, res_ref,
-    w, ext, adj, sc, masked, img, image2, dirn, es, er, ts, tr, ar0, ar1, packed,
+    w, ext, adj, sc, masked, img, image2, dirn, es, er, ts, tr, vown, vhalo, ar0, ar1, packed,
     kap_ref, inv_ref, mask_ref, prec_ref, tsem, wsem, send_sem, recv_sem, ar_send, ar_recv,
 ):
     rows, nk, cols = rhs_ref.shape
@@ -102,10 +102,12 @@
 
     def pair(it, kind):
         if kind == HALO:
-            own = ext.at[it, pl.ds(rows, rows)]
+            if it == 1:
+                return tuple(copy(it, kind, d, vown, vhalo.at[d]) for d in range(2))
+            own = ext.at[pl.ds(rows, rows)]
             return (
-                copy(it, kind, 0, own, ext.at[it, pl.ds(0, rows)]),
-                copy(it, kind, 1, own, ext.at[it, pl.ds(2 * rows, rows)]),
+                copy(it, kind, 0, own, ext.at[pl.ds(0, rows)]),
+                copy(it, kind, 1, own, ext.at[pl.ds(2 * rows, rows)]),
             )
         if kind >= TERMS:
             h = kind - TERMS
@@ -127,8 +129,9 @@
 
     @pl.when(jnp.logical_not(has_up))
     def _():
+        ext[pl.ds(0, rows)] = jnp.zeros((rows, nk, cols), jnp.bfloat16)
+        vhalo[0] = jnp.zeros((rows, nk, cols), jnp.bfloat16)
         for it in range(2):
-            ext[it, pl.ds(0, rows)] = jnp.zeros((rows, nk, cols), jnp.bfloat16)
             for h in range(HALVES):
                 tr[it, h, 0] = jnp.zeros((rows, nk, half), jnp.bfloat16)
             for e in range(2):
@@ -136,8 +139,9 @@
 
     @pl.when(jnp.logical_not(has_down))
     def _():
+        ext[pl.ds(2 * rows, rows)] = jnp.zeros((rows, nk, cols), jnp.bfloat16)
+        vhalo[1] = jnp.zeros((rows, nk, cols), jnp.bfloat16)
         for it in range(2):
-            ext[it, pl.ds(2 * rows, rows)] = jnp.zeros((rows, nk, cols), jnp.bfloat16)
             for h in range(HALVES):
                 tr[it, h, 1] = jnp.zeros((rows, nk, half), jnp.bfloat16)
             for e in range(2):
@@ -170,16 +174,19 @@
         masked[0] = er[it, e, 0].astype(jnp.float32)
         masked[rows + 1] = er[it, e, 1].astype(jnp.float32)
 
-    def apply(it, field, out):
+    def apply(it, field, out, make_halo=None):
         for r in range(rows):
             masked[r + 1] = at(maskf, r) * field[r]
-            ext[it, rows + r] = field[r].astype(jnp.bfloat16)
+            ext[rows + r] = field[r].astype(jnp.bfloat16)
         stage_edges(it, 0)
         if it == 0:
             down, up = (jnp.where(x, 1, 0) for x in (has_down, has_up))
             pl.semaphore_wait(barrier, count + down + up)
         start(it, FIELD_EDGE)
-        start(it, HALO)
+        if make_halo is None:
+            start(it, HALO)
+        else:
+            make_halo()
         arrive(it, FIELD_EDGE)
         take_edges(it, 0)
         for r in range(rows):
@@ -189,14 +196,15 @@
             masked[r + 1] = at(maskf, r) * out[r]
         stage_edges(it, 1)
         start(it, INNER_EDGE)
-        arrive(it, HALO)
+        if make_halo is None:
+            arrive(it, HALO)
 
         def observe(t, carry):
             if it == 0:
                 pltpu.make_async_copy(w_hbm.at[t], w.at[t], wsem.at[t]).wait()
             total = jnp.zeros((nk, obs), jnp.float32)
             for j in range(foot):
-                x = ext[it, idx_ref[t * foot + j]]
+                x = ext[idx_ref[t * foot + j]]
                 total += dot(x, w[t, j], NT, None)
             sc[t] = (prec_ref[pl.ds(t, 1), :] * total).astype(jnp.bfloat16)
             return carry
@@ -236,6 +244,10 @@
             for r in range(rows):
                 beyond = tr[it, h, 0, r].astype(jnp.float32) + tr[it, h, 1, r].astype(jnp.float32)
                 out[r, :, part] += adj[h, idx_ref[2 * picks + rows + r]] + beyond
+        if it == 0:
+            for r in range(rows):
+                vown[r] = out[r].astype(jnp.bfloat16)
+            start(1, HALO)
         for kind in range(KINDS):
             drain(it, kind)
 
@@ -330,7 +342,22 @@
         res_ref[r] = left
         dirn[r] = left + all_three[2 * nk :]
 
-    apply(1, dirn, image2)
+    high, low = halves_of(jnp.concatenate([mix_t, -step_t], axis=1))
+    beyond_t = jnp.concatenate([high, low], axis=1)
+
+    def beyond_direction():
+        arrive(1, HALO)
+        for d in range(2):
+            def one(r, carry):
+                x = ext[2 * rows * d + r]
+                y = vhalo[d, r]
+                new = dot(beyond_t, jnp.concatenate([x, y, x, y], axis=0), NN, None)
+                ext[2 * rows * d + r] = (x.astype(jnp.float32) + new).astype(jnp.bfloat16)
+                return carry
+
+            lax.fori_loop(0, rows, one, 0, unroll=4)
+
+    apply(1, dirn, image2, beyond_direction)
     total = pack(dirn, image2)
     total = 0.5 * (total[:nk, nk:] + total[nk:, :nk])
     fold = nk // 4
@@ -384,7 +411,7 @@
         out_specs=[vmem] * 2,
         scratch_shapes=[
             pltpu.VMEM(weights.shape, bf16),
-            pltpu.VMEM((2, 3 * rows, nk, cols), bf16),
+            pltpu.VMEM((3 * rows, nk, cols), bf16),
             pltpu.VMEM((HALVES, picks + 1, nk, half), f32),
             pltpu.VMEM((tiles, nk, obs), bf16),
             pltpu.VMEM((rows + 2, nk, cols), f32),
@@ -395,6 +422,8 @@
             pltpu.VMEM((2, 2, 2, nk, cols), bf16),
             pltpu.VMEM((2, HALVES, 2, rows, nk, half), bf16),
             pltpu.VMEM((2, HALVES, 2, rows, nk, half), bf16),
+            pltpu.VMEM(field, bf16),
+            pltpu.VMEM((2,) + field, bf16),
             pltpu.VMEM((levels, RADIX, nk, 4 * nk), f32),
             pltpu.VMEM((levels, RADIX, nk // 4, 4 * nk), f32),
             pltpu.VMEM((rows, 4 * nk, cols), bf16),
@@ -410,7 +439,7 @@
             pltpu.SemaphoreType.DMA((2, levels, RADIX)),
         ],
         compiler_params=pltpu.CompilerParams(
-            collective_id=0, has_side_effects=True, vmem_limit_bytes=60 * 1024 * 1024
+            collective_id=0, has_side_effects=True, vmem_limit_bytes=50 * 1024 * 1024
         ),
     )(
         jnp.swapaxes(right_sides, 0, 1),

time: 99.6 us -> 98.4 us (0.988)
    unnamed x3 -> x11, local copies, waits for them, and re-layouts: 8.41 us -> 7.96 us
where the time goes in v3:
time: 98.4 us; the launch traced here: 97.9 us
  Pallas kernels  87.6 us (89%)
  local copies, waits for them, and re-layouts  8.04 us (8%)
  other arithmetic  1.6 us (2%)
    pallas_call x1, Pallas kernels, body(): pl.pallas_call(functools.partial(kernel, n), out_shape=[jax.ShapeDtypeStr...  87.6 us
    unnamed x11, local copies, waits for them, and re-layouts  7.96 us

profile of v3, /device:TPU:0, one launch (start us, length us, event | category | flops | bytes accessed | tf_op | source)
XLA Modules:
  0.0 97.9 jit_solution(12035867744371619584)
XLA Ops:
  0.7 0.7 broadcast_subtract_fusion
  1.3 0.1 reshape.15
  1.4 0.1 pad_add_fusion.1
  1.5 0.8 select_reduce_fusion
  2.3 0.1 pad_add_fusion.idx_ref
  2.3 1.8 %copy.16 = f32[32,16,512]{2,0,1:T(8,128)S(1)} copy(f32[32,16,512]{2,1,0:T(8,128)} %param.7) | data formatting | bytes 2097152 | tf_op args[0]
  4.2 0.0 copy-start
  4.2 0.7 copy-done
  4.9 0.0 copy-start.1
  4.9 0.8 copy-done.1
  5.7 0.0 copy-start.2
  5.7 0.8 copy-done.2
  6.5 0.0 copy-start.3
  6.5 0.7 copy-done.3
  7.1 87.6 %shard_map.86 = (f32[16,32,512]{2,1,0:T(8,128)S(1)}, f32[16,32,512]{2,1,0:T(8,128)S(1)}) custom-call(f32[16,32,512]{2,1,0:T(8,128)S(1)} %bitcast.5, f32[16,512]{1,0:T(8,128)S(1)} %copy-done, f32[16,512]{1,0:T(8,128)S(1)} %copy-done.1, s32[16,512]{1,0:T(8,128)S(1)} %copy-done.2, bf16[8,8,128,512]{3,2,1,0:T(8,128)(2,1)} %w_hbm.1, f32[8,128]{1,0:T(8,128)S(1)} %copy-done.3, ...), custom_call_target="tpu_custom_call" | custom-call | tf_op jit(solution)/shard_map/pallas_call | solution.py:405
  94.8 1.6 %copy.13 = f32[32,16,512]{2,1,0:T(8,128)} copy(f32[32,16,512]{2,0,1:T(8,128)S(1)} %bitcast.7) | data formatting | bytes 2097152
  96.3 1.6 %copy.14 = f32[32,16,512]{2,1,0:T(8,128)} copy(f32[32,16,512]{2,0,1:T(8,128)S(1)} %bitcast.6) | data formatting | bytes 2097152
  (2 shorter events, 0.0 us)
Async XLA Ops:
  4.2 0.8 copy-start
  4.9 0.8 copy-start.1
  5.7 0.8 copy-start.2
  6.5 0.7 copy-start.3

commit v4 on v3

--- a/solution.py
+++ b/solution.py
@@ -187,12 +187,20 @@
             start(it, HALO)
         else:
             make_halo()
+        inside = list(range(1, rows - 1))
+        ends = [0, rows - 1]
+
+        def inner(r):
+            value = at(kap, r) * field[r] + at(maskf, r) * (4.0 * field[r] - beside(r))
+            out[r] = at(inv, r) * value
+
+        for r in inside:
+            inner(r)
         arrive(it, FIELD_EDGE)
         take_edges(it, 0)
+        for r in ends:
+            inner(r)
         for r in range(rows):
-            out[r] = at(kap, r) * field[r] + at(maskf, r) * (4.0 * field[r] - beside(r))
-        for r in range(rows):
-            out[r] = at(inv, r) * out[r]
             masked[r + 1] = at(maskf, r) * out[r]
         stage_edges(it, 1)
         start(it, INNER_EDGE)
@@ -247,7 +255,6 @@
         if it == 0:
             for r in range(rows):
                 vown[r] = out[r].astype(jnp.bfloat16)
-            start(1, HALO)
         for kind in range(KINDS):
             drain(it, kind)
 
@@ -276,7 +283,7 @@
 
         return row
 
-    def reduce_all(which, ar, value):
+    def reduce_all(which, ar, value, meanwhile=None):
         for lv, (stride, radix) in enumerate(levels):
             q = lax.rem(me // stride, radix)
             ar[lv, q] = value
@@ -293,6 +300,8 @@
             ]
             for c in copies:
                 c.start()
+            if meanwhile is not None and lv == 0:
+                meanwhile()
             for c in copies:
                 c.wait_recv()
             for c in copies:
@@ -312,7 +321,8 @@
 
     apply(0, rhs_ref, img)
     total = pack(rhs_ref, img)
-    total = reduce_all(0, ar0, jnp.concatenate([total[:nk], total[nk:]], axis=1))
+    total = jnp.concatenate([total[:nk], total[nk:]], axis=1)
+    total = reduce_all(0, ar0, total, lambda: start(1, HALO))
     g00, g01, g10, g11 = (total[:, p * nk : (p + 1) * nk] for p in range(4))
     first, second = eliminate(
         [
@@ -406,7 +416,7 @@
         functools.partial(kernel, n),
         out_shape=[jax.ShapeDtypeStruct(field, f32)] * 2,
         in_specs=[vmem]
-        + [pl.BlockSpec(memory_space=pl.ANY)] * 5
+        + [pl.BlockSpec(memory_space=pltpu.HBM)] * 5
         + [pl.BlockSpec(memory_space=pltpu.SMEM)],
         out_specs=[vmem] * 2,
         scratch_shapes=[

time: 98.4 us -> 93.1 us (0.946)
  Pallas kernels: 87.6 us -> 82.4 us
    pallas_call x1, Pallas kernels: 87.6 us -> 82.4 us  [body(): pl.pallas_call(functools.partial(kernel, n), out_shape=[jax.ShapeDtypeStr...]
where the time goes in v4:
time: 93.1 us; the launch traced here: 92.7 us
  Pallas kernels  82.4 us (89%)
  local copies, waits for them, and re-layouts  8.04 us (9%)
  other arithmetic  1.6 us (2%)
    pallas_call x1, Pallas kernels, body(): pl.pallas_call(functools.partial(kernel, n), out_shape=[jax.ShapeDtypeStr...  82.4 us
    unnamed x11, local copies, waits for them, and re-layouts  7.96 us

profile of v4, /device:TPU:0, one launch (start us, length us, event | category | flops | bytes accessed | tf_op | source)
XLA Modules:
  0.0 92.7 jit_solution(14204241598585797776)
XLA Ops:
  0.7 0.7 broadcast_subtract_fusion
  1.3 0.1 reshape.15
  1.4 0.1 pad_add_fusion.1
  1.5 0.8 select_reduce_fusion
  2.3 0.1 pad_add_fusion.idx_ref
  2.3 1.8 %copy.16 = f32[32,16,512]{2,0,1:T(8,128)S(1)} copy(f32[32,16,512]{2,1,0:T(8,128)} %param.7) | data formatting | bytes 2097152 | tf_op args[0]
  4.2 0.0 copy-start
  4.2 0.7 copy-done
  4.9 0.0 copy-start.1
  4.9 0.8 copy-done.1
  5.7 0.0 copy-start.2
  5.7 0.8 copy-done.2
  6.5 0.0 copy-start.3
  6.5 0.7 copy-done.3
  7.1 82.4 %shard_map.86 = (f32[16,32,512]{2,1,0:T(8,128)S(1)}, f32[16,32,512]{2,1,0:T(8,128)S(1)}) custom-call(f32[16,32,512]{2,1,0:T(8,128)S(1)} %bitcast.5, f32[16,512]{1,0:T(8,128)S(1)} %copy-done, f32[16,512]{1,0:T(8,128)S(1)} %copy-done.1, s32[16,512]{1,0:T(8,128)S(1)} %copy-done.2, bf16[8,8,128,512]{3,2,1,0:T(8,128)(2,1)} %w_hbm.1, f32[8,128]{1,0:T(8,128)S(1)} %copy-done.3, ...), custom_call_target="tpu_custom_call" | custom-call | tf_op jit(solution)/shard_map/pallas_call | solution.py:415
  89.5 1.6 %copy.13 = f32[32,16,512]{2,1,0:T(8,128)} copy(f32[32,16,512]{2,0,1:T(8,128)S(1)} %bitcast.7) | data formatting | bytes 2097152
  91.1 1.6 %copy.14 = f32[32,16,512]{2,1,0:T(8,128)} copy(f32[32,16,512]{2,0,1:T(8,128)S(1)} %bitcast.6) | data formatting | bytes 2097152
  (2 shorter events, 0.0 us)
Async XLA Ops:
  4.2 0.8 copy-start
  4.9 0.8 copy-start.1
  5.7 0.8 copy-start.2
  6.5 0.7 copy-start.3

commit v5 on v4

--- a/solution.py
+++ b/solution.py
@@ -43,10 +43,10 @@
 
 def kernel(
     n,
-    rhs_ref, kap_hbm, inv_hbm, mask_hbm, w_hbm, prec_hbm, idx_ref,
+    rhs_ref, tables_ref, w_hbm, idx_ref,
     sol_ref, res_ref,
     w, ext, adj, sc, masked, img, image2, dirn, es, er, ts, tr, vown, vhalo, ar0, ar1, packed,
-    kap_ref, inv_ref, mask_ref, prec_ref, tsem, wsem, send_sem, recv_sem, ar_send, ar_recv,
+    wsem, send_sem, recv_sem, ar_send, ar_recv,
 ):
     rows, nk, cols = rhs_ref.shape
     tiles, foot, obs, _ = w.shape
@@ -56,14 +56,6 @@
     levels = radices(n)
 
     half = cols // HALVES
-    tables = [
-        pltpu.make_async_copy(src, dst, tsem.at[i])
-        for i, (src, dst) in enumerate(
-            ((kap_hbm, kap_ref), (inv_hbm, inv_ref), (mask_hbm, mask_ref), (prec_hbm, prec_ref))
-        )
-    ]
-    for c in tables:
-        c.start()
     for t in range(tiles):
         pltpu.make_async_copy(w_hbm.at[t], w.at[t], wsem.at[t]).start()
 
@@ -149,13 +141,9 @@
 
     for h in range(HALVES):
         adj[h, 0] = jnp.zeros((nk, half), jnp.float32)
-    for c in tables:
-        c.wait()
 
     lane = lax.broadcasted_iota(jnp.int32, (nk, cols), 1)
-    maskf = mask_ref[...].astype(jnp.float32)
-    kap = kap_ref[...]
-    inv = inv_ref[...]
+    kap, inv, maskf = (tables_ref[pl.ds(p * rows, rows), :] for p in range(3))
 
     def at(table, r):
         return table[r : r + 1, :]
@@ -214,7 +202,7 @@
             for j in range(foot):
                 x = ext[idx_ref[t * foot + j]]
                 total += dot(x, w[t, j], NT, None)
-            sc[t] = (prec_ref[pl.ds(t, 1), :] * total).astype(jnp.bfloat16)
+            sc[t] = (tables_ref[pl.ds(3 * rows + t, 1), :][:, :obs] * total).astype(jnp.bfloat16)
             return carry
 
         lax.fori_loop(0, tiles, observe, 0, unroll=2)
@@ -407,6 +395,15 @@
     last = jnp.max(jnp.where(same, order[None, :] + 1, 0), axis=1)
     index = jnp.concatenate([ids, last])
 
+    tables = jnp.concatenate(
+        [
+            kappa_sq,
+            inv_mass,
+            cell_mask.astype(jnp.float32),
+            jnp.pad(obs_precision, ((0, 0), (0, cols - obs))),
+        ],
+        axis=0,
+    )
     levels = len(radices(n))
     half = cols // HALVES
     field = (rows, nk, cols)
@@ -416,7 +413,7 @@
         functools.partial(kernel, n),
         out_shape=[jax.ShapeDtypeStruct(field, f32)] * 2,
         in_specs=[vmem]
-        + [pl.BlockSpec(memory_space=pltpu.HBM)] * 5
+        + [vmem, pl.BlockSpec(memory_space=pltpu.HBM)]
         + [pl.BlockSpec(memory_space=pltpu.SMEM)],
         out_specs=[vmem] * 2,
         scratch_shapes=[
@@ -437,11 +434,6 @@
             pltpu.VMEM((levels, RADIX, nk, 4 * nk), f32),
             pltpu.VMEM((levels, RADIX, nk // 4, 4 * nk), f32),
             pltpu.VMEM((rows, 4 * nk, cols), bf16),
-            pltpu.VMEM(kappa_sq.shape, f32),
-            pltpu.VMEM(inv_mass.shape, f32),
-            pltpu.VMEM(cell_mask.shape, jnp.int32),
-            pltpu.VMEM(obs_precision.shape, f32),
-            pltpu.SemaphoreType.DMA((4,)),
             pltpu.SemaphoreType.DMA((tiles,)),
             pltpu.SemaphoreType.DMA((2, KINDS, 2)),
             pltpu.SemaphoreType.DMA((2, KINDS, 2)),
@@ -453,11 +445,8 @@
         ),
     )(
         jnp.swapaxes(right_sides, 0, 1),
-        kappa_sq,
-        inv_mass,
-        cell_mask,
+        tables,
         weights,
-        obs_precision,
         index,
     )
     return (jnp.swapaxes(solved, 0, 1), jnp.swapaxes(left, 0, 1))

time: 93.1 us -> 91.5 us (0.983)
  local copies, waits for them, and re-layouts: 8.04 us -> 5.08 us
  other arithmetic: 1.6 us -> 3.17 us
    unnamed x11 -> x3, local copies, waits for them, and re-layouts: 7.96 us -> 5 us
where the time goes in v5:
time: 91.5 us; the launch traced here: 91.1 us
  Pallas kernels  82.2 us (90%)
  local copies, waits for them, and re-layouts  5.08 us (6%)
  other arithmetic  3.17 us (3%)
    pallas_call x1, Pallas kernels, body(): pl.pallas_call(functools.partial(kernel, n), out_shape=[jax.ShapeDtypeStr...  82.2 us
    unnamed x3, local copies, waits for them, and re-layouts  5 us

profile of v5, /device:TPU:0, one launch (start us, length us, event | category | flops | bytes accessed | tf_op | source)
XLA Modules:
  0.0 91.1 jit_solution(6893773597906055916)
XLA Ops:
  0.7 0.7 broadcast_subtract_fusion
  1.3 0.1 reshape.15
  1.4 0.1 pad_add_fusion.1
  1.5 0.8 select_reduce_fusion
  2.3 0.1 pad_add_fusion.idx_ref
  2.3 0.8 convert_element_type.5
  3.1 0.8 select_maximum_fusion.tables_ref
  3.9 1.8 %copy.16 = f32[32,16,512]{2,0,1:T(8,128)S(1)} copy(f32[32,16,512]{2,1,0:T(8,128)} %param.7) | data formatting | bytes 2097152 | tf_op args[0]
  5.7 82.2 %shard_map.86 = (f32[16,32,512]{2,1,0:T(8,128)S(1)}, f32[16,32,512]{2,1,0:T(8,128)S(1)}) custom-call(f32[16,32,512]{2,1,0:T(8,128)S(1)} %bitcast.5, f32[56,512]{1,0:T(8,128)S(1)} %select_maximum_fusion.tables_ref, bf16[8,8,128,512]{3,2,1,0:T(8,128)(2,1)} %w_hbm.1, s32[176]{0:T(256)S(1)} %pad_add_fusion.idx_ref), custom_call_target="tpu_custom_call" | custom-call | tf_op jit(solution)/shard_map/pallas_call | solution.py:412
  88.0 1.6 %copy.13 = f32[32,16,512]{2,1,0:T(8,128)} copy(f32[32,16,512]{2,0,1:T(8,128)S(1)} %bitcast.7) | data formatting | bytes 2097152
  89.6 1.6 %copy.14 = f32[32,16,512]{2,1,0:T(8,128)} copy(f32[32,16,512]{2,0,1:T(8,128)S(1)} %bitcast.6) | data formatting | bytes 2097152
  (2 shorter events, 0.0 us)
